TPU v7x, 32 devices: a whole 2x2x4 slice. The times are simulated.
32 devices in a mesh: req: 16 (over z, y, x), head: 2 (over core).
Axes of the slice: x: 2, y: 2, z: 4, core: 2. Of those that a mesh axis runs over, the one named last changes fastest.
Arguments:
- queries: bfloat16 [2, 16, 128, 576], P(None, 'req', 'head'), may hold values from -100 to 100
- prompt_cache: bfloat16 [8192, 576], P('req'), may hold values from -10 to 10
- suffix_cache: bfloat16 [16, 8, 64, 576], P('req'), may hold values from -14 to 14
- new_latent: bfloat16 [2, 16, 576], P(None, 'req'), may hold values from -16 to 16
- suffix_len: int32 [16], P('req'), may hold values from 1 to 512, 4352 in all
- parent: int32 [16], P('req'), may hold values from 0 to 15
- fork_pages: int32 [16, 2], P('req'), may hold values from 0 to 7
Outputs:
- attended: bfloat16 [2, 16, 128, 512], P(None, 'req', 'head')
Inputs may be any that keep to these rules, and one draw needn't show every extreme that they name: `suffix_len`: every beam has at least one valid own token.
All inputs are finite; a program needn't handle non-finite values. No bound on the sum of `suffix_len` on one device may be relied on, other than what follows from the above.
Results may differ from a plain program's by a relative error of at most 0.008.
Values may be sent and summed in bfloat16 or wider, within the bound.
A program may use at most 64 MiB of HBM per device.

v0:
```python
import math

import jax
import jax.numpy as jnp
from jax import lax
from jax.sharding import PartitionSpec as P

DL = 512


score_scale = 192.0 ** (-0.5)
neg_large = -1e30


def prompt_block(rows, keys):
    scores = (
        lax.dot_general(rows, keys, (((1,), (1,)), ((), ())), preferred_element_type=jnp.float32)
        * score_scale
    )
    top = jnp.max(scores, axis=-1)
    weights = jnp.exp(scores - top[:, None])
    total = jnp.sum(weights, axis=-1)
    summed = jnp.dot(weights.astype(jnp.bfloat16), keys[:, :DL], preferred_element_type=jnp.float32)
    return (top, total, (summed / total[:, None]).astype(jnp.bfloat16))


def masked_partial(queries, keys, valid):
    scores = (
        jnp.einsum("sbhk,btk->sbht", queries, keys, preferred_element_type=jnp.float32)
        * score_scale
    )
    scores = jnp.where(valid, scores, neg_large)
    top = jnp.max(scores, axis=-1)
    weights = jnp.where(valid, jnp.exp(scores - top[..., None]), 0.0)
    total = jnp.sum(weights, axis=-1)
    summed = jnp.einsum(
        "sbht,btd->sbhd",
        weights.astype(jnp.bfloat16),
        keys[..., :DL],
        preferred_element_type=jnp.float32,
    )
    return (top, total, summed)


def finish_fork(total, summed):
    return (summed / jnp.maximum(total, 1.0)[..., None]).astype(jnp.bfloat16)


def combine_parts(top_pr, total_pr, out_pr, top_fr, total_fr, out_fr, top_l, total_l, summed_l):
    peak = jnp.maximum(jnp.maximum(jnp.max(top_pr, axis=1), jnp.max(top_fr, axis=1)), top_l)
    weight_p = total_pr * jnp.exp(top_pr - peak[:, None])
    weight_f = total_fr * jnp.exp(top_fr - peak[:, None])
    weight_l = jnp.exp(top_l - peak)
    denom = jnp.sum(weight_p, axis=1) + jnp.sum(weight_f, axis=1) + total_l * weight_l
    numer = (
        jnp.sum(weight_p[..., None] * out_pr, axis=1)
        + jnp.sum(weight_f[..., None] * out_fr, axis=1)
        + weight_l[..., None] * summed_l
    )
    return numer / denom[..., None]


def on_device(queries, prompt_cache, suffix_cache, new_latent, suffix_len, parent, fork_pages):
    steps_n, beam_dev, head_dev, width = queries.shape
    pages_n, page_len = (suffix_cache.shape[1], suffix_cache.shape[2])
    forks_n = fork_pages.shape[1]
    req_n = lax.axis_size("req")
    first_beam = lax.axis_index("req") * beam_dev
    every_query = lax.all_gather(queries, "req", axis=1, tiled=True)
    all_parent, all_pages, all_len = (
        lax.all_gather(parent, "req", axis=0, tiled=True),
        lax.all_gather(fork_pages, "req", axis=0, tiled=True),
        lax.all_gather(suffix_len, "req", axis=0, tiled=True),
    )
    beams_n = every_query.shape[1]
    rows_n = steps_n * beams_n * head_dev
    block = math.gcd(rows_n, 512)
    blocks = every_query.reshape(rows_n // block, block, width)
    top_p, total_p, out_p = lax.map(lambda rows: prompt_block(rows, prompt_cache), blocks)
    top_p = top_p.reshape(steps_n, beams_n, head_dev)
    total_p = total_p.reshape(steps_n, beams_n, head_dev)
    out_p = out_p.reshape(steps_n, beams_n, head_dev, DL)
    local_parent = all_parent - first_beam
    owned = (local_parent >= 0) & (local_parent < beam_dev)
    source_beam = jnp.clip(local_parent, 0, beam_dev - 1)
    picked = suffix_cache[source_beam[:, None], all_pages]
    offsets = jnp.arange(page_len, dtype=jnp.int32)
    own_keys = jnp.concatenate(
        [suffix_cache.reshape(beam_dev, pages_n * page_len, width), jnp.swapaxes(new_latent, 0, 1)],
        axis=1,
    )
    old_valid = jnp.arange(pages_n * page_len, dtype=jnp.int32)[None, :] < suffix_len[:, None]
    new_valid = (
        jnp.arange(steps_n, dtype=jnp.int32)[None, :]
        <= jnp.arange(steps_n, dtype=jnp.int32)[:, None]
    )
    own_valid = jnp.concatenate(
        [
            jnp.broadcast_to(old_valid[None], (steps_n, beam_dev, pages_n * page_len)),
            new_valid[:, None, :],
        ],
        axis=2,
    )[:, :, None, :]
    top_l, total_l, summed_l = masked_partial(queries, own_keys, own_valid)
    outgoing = jnp.where(owned[:, None, None, None], picked, jnp.zeros_like(picked))
    arrived = lax.all_to_all(outgoing, "req", split_axis=0, concat_axis=0, tiled=True)
    tiles = jnp.sum(arrived.reshape(req_n, beam_dev, forks_n, page_len, width), axis=0)
    tiles = tiles.reshape(beam_dev, forks_n * page_len, width)
    positions = (fork_pages[:, :, None] * page_len + offsets[None, None, :]).reshape(beam_dev, -1)
    fork_valid = (positions < all_len[parent][:, None])[None, :, None, :]
    top_f, total_f, summed_f = masked_partial(queries, tiles, fork_valid)
    out_f = finish_fork(total_f, summed_f).astype(jnp.float32)
    out_pr, top_pr, total_pr = (
        lax.all_to_all(
            out_p.astype(jnp.float32), "req", split_axis=1, concat_axis=1, tiled=True
        ).astype(out_p.dtype),
        lax.all_to_all(top_p, "req", split_axis=1, concat_axis=1, tiled=True),
        lax.all_to_all(total_p, "req", split_axis=1, concat_axis=1, tiled=True),
    )
    top_pr = top_pr.reshape(steps_n, req_n, beam_dev, head_dev)
    total_pr = total_pr.reshape(steps_n, req_n, beam_dev, head_dev)
    out_pr = out_pr.astype(jnp.float32).reshape(steps_n, req_n, beam_dev, head_dev, DL)
    result = combine_parts(
        top_pr,
        total_pr,
        out_pr,
        top_f[:, None],
        total_f[:, None],
        out_f[:, None],
        top_l,
        total_l,
        summed_l,
    )
    return result.astype(jnp.bfloat16)


def solution(mesh):
    placed = (
        P(None, "req", "head", None),
        P("req", None),
        P("req", None, None, None),
        P(None, "req", None),
        P("req"),
        P("req"),
        P("req", None),
    )
    return jax.shard_map(
        on_device,
        mesh=mesh,
        in_specs=placed,
        out_specs=P(None, "req", "head", None),
        check_vma=False,
    )
```

profile of v0, /device:TPU:12, one launch (start us, length us, event | category | flops | bytes accessed | tf_op | source)
XLA Modules:
  0.0 209.4 jit_solution(17603017229917052786)
XLA Ops:
  6.5 0.7 all-gather.3.cloned.1.call-update
  7.9 30.8 %all-gather = s32[16,1,2]{2,1,0:T(1,128)S(1)} all-gather(s32[1,1,2]{2,1,0:T(1,128)} %bitcast.164), channel_id=1, replica_groups=mesh['req'=16,'head'=2] {'req'}, dimensions={0}, use_global_device_ids=true | all-gather | bytes 136 | tf_op jit(solution)/shard_map/all_gather | solution.py:72
  39.5 1.3 dynamic-slice.3
  40.8 0.8 dynamic-update-slice.2
  41.6 0.8 dynamic-update-slice.1
  42.4 20.0 %all-reduce.2 = (s32[16]{0:T(128)S(1)}, s32[16]{0:T(128)S(1)}) all-reduce(s32[16]{0:T(128)S(1)} %dynamic-update-slice.2, s32[16]{0:T(128)S(1)} %dynamic-update-slice.1), channel_id=1, replica_groups=mesh['req'=16,'head'=2] {'req'}, use_global_device_ids=true, to_apply=%add.1 | all-reduce | flops 32 | bytes 256
  62.4 0.1 copy.23
  62.5 0.1 reshape.321
  62.6 2.1 %gather_fusion = bf16[32,64,576]{2,1,0:T(8,128)(2,1)S(1)} fusion(bf16[1,8,64,576]{3,2,1,0:T(8,128)(2,1)} %param.11, s32[32]{0:T(128)S(1)} %reshape.321), kind=kCustom, calls=%fused_computation | custom fusion | bytes 4718848 | tf_op jit(solution)/shard_map/gather | solution.py:86
  64.7 1.8 broadcast_select_fusion
  66.5 7.0 %all-to-all-start.2 = ((bf16[16,2,64,576]{3,2,1,0:T(8,128)(2,1)}), bf16[16,2,64,576]{3,2,1,0:T(8,128)(2,1)}, u32[]{:S(2)}, u32[]{:S(2)}) async-start(bf16[16,2,64,576]{3,2,1,0:T(8,128)(2,1)} %broadcast_select_fusion), calls=%async_computation.2 | async-start | bytes 5242880 | tf_op jit(solution)/shard_map/all_to_all | solution.py:106
  73.6 10.9 %all-gather.3.cloned.1.call-done = bf16[2,16,64,576]{3,2,1,0:T(8,128)(2,1)} async-done(((bf16[2,1,64,576]{3,2,1,0:T(8,128)(2,1)}), bf16[2,16,64,576]{3,2,1,0:T(8,128)(2,1)}) %all-gather.3.cloned.1.call-update) | async-done | bytes 2359312 | tf_op jit(solution)/shard_map/all_gather | solution.py:69
  84.4 13.4 %while.15 = (s32[]{:T(128)}, f32[4,512]{1,0:T(4,128)S(1)}, f32[4,512]{1,0:T(4,128)S(1)}, bf16[4,512,512]{2,1,0:T(8,128)(2,1)}, bf16[4,512,576]{2,1,0:T(8,128)(2,...) while((s32[]{:T(128)}, f32[4,512]{1,0:T(4,128)S(1)}, f32[4,512]{1,0:T(4,128)S(1)}, ...), condition=%wide.region_3.4_spmd, body=%wide.region_0.3_spmd.sunk | while | flops 572521472 | bytes 5458029 | solution.py:79
  84.4 1.7 fusion.73
  86.2 0.2 fusion.74
  86.5 1.3 fusion.75
  87.8 1.7 fusion.73
  89.6 0.2 fusion.74
  89.8 1.4 fusion.75
  91.2 1.7 fusion.73
  92.9 0.2 fusion.74
  93.2 1.4 fusion.75
  94.5 1.7 fusion.73
  96.3 0.2 fusion.74
  96.6 1.3 fusion.75
  98.0 0.7 reshape.351
  98.6 30.9 %all-to-all-done.2 = bf16[16,2,64,576]{3,2,1,0:T(8,128)(2,1)} async-done(((bf16[16,2,64,576]{3,2,1,0:T(8,128)(2,1)}), bf16[16,2,64,576]{3,2,1,0:T(8,128)(2,1)}, u32[]{:S(2)}, u32[]{:S(2)}) %all-to-all-start.2) | async-done | bytes 2359328 | tf_op jit(solution)/shard_map/all_to_all | solution.py:106
  129.6 5.5 %all-to-all-start.1 = ((f32[16,1,128]{2,1,0:T(1,128)}), f32[16,1,128]{2,1,0:T(1,128)S(1)}, u32[]{:S(2)}, u32[]{:S(2)}) async-start(f32[16,1,128]{2,1,0:T(1,128)} %reshape.351), calls=%async_computation.1 | async-start | bytes 16384 | tf_op jit(solution)/shard_map/all_to_all | solution.py:117
  135.2 0.7 reshape.349
  135.8 4.2 %all-to-all-done.1 = f32[16,1,128]{2,1,0:T(1,128)S(1)} async-done(((f32[16,1,128]{2,1,0:T(1,128)}), f32[16,1,128]{2,1,0:T(1,128)S(1)}, u32[]{:S(2)}, u32[]{:S(2)}) %all-to-all-start.1) | async-done | bytes 8224 | tf_op jit(solution)/shard_map/all_to_all | solution.py:117
  140.0 5.5 %all-to-all-start = ((f32[16,1,128]{2,1,0:T(1,128)}), f32[16,1,128]{2,1,0:T(1,128)S(1)}, u32[]{:S(2)}, u32[]{:S(2)}) async-start(f32[16,1,128]{2,1,0:T(1,128)} %reshape.349), calls=%async_computation | async-start | bytes 16384 | tf_op jit(solution)/shard_map/all_to_all | solution.py:118
  145.6 3.1 %copy.25 = bf16[2,16,64,512]{3,2,0,1:T(8,128)(2,1)} copy(bf16[2,16,64,512]{3,2,1,0:T(8,128)(2,1)} %bitcast.157) | data formatting | bytes 4194304 | tf_op jit(solution)/shard_map/convert_element_type | solution.py:115
  148.7 2.0 all-to-all-done
  150.7 5.9 %all-to-all-start.3 = ((bf16[2,16,64,512]{3,2,0,1:T(8,128)(2,1)}), bf16[2,16,64,512]{3,2,0,1:T(8,128)(2,1)S(1)}, u32[]{:S(2)}, u32[]{:S(2)}) async-start(bf16[2,16,64,512]{3,2,0,1:T(8,128)(2,1)} %copy.25), calls=%async_computation.3 | async-start | bytes 4194304 | tf_op jit(solution)/shard_map/all_to_all | solution.py:114
  156.8 0.6 dynamic-slice.2
  157.4 0.5 fusion.60
  157.9 0.2 fusion.34
  158.1 0.6 add_compare_fusion
  158.7 2.2 %reduce_sum.67 = bf16[2,64,576]{2,1,0:T(8,128)(2,1)S(1)} reduce(bf16[16,2,64,576]{3,2,1,0:T(8,128)(2,1)} %all-to-all-done.2, bf16[]{:T(256)} %constant.15.clone.1), dimensions={0}, to_apply=%region_5.6 | reduce | flops 1105920 | bytes 2506754 | tf_op jit(solution)/shard_map/reduce_sum | solution.py:107
  160.8 0.3 fusion.61
  161.1 0.2 fusion.44
  161.3 0.5 broadcast.151
  161.8 0.7 reduce.13
  162.6 0.7 reduce.14
  163.4 37.4 %all-to-all-done.3 = bf16[2,16,64,512]{3,2,0,1:T(8,128)(2,1)S(1)} async-done(((bf16[2,16,64,512]{3,2,0,1:T(8,128)(2,1)}), bf16[2,16,64,512]{3,2,0,1:T(8,128)(2,1)S(1)}, u32[]{:S(2)}, u32[]{:S(2)}) %all-to-all-start.3) | async-done | bytes 2097184 | tf_op jit(solution)/shard_map/all_to_all | solution.py:114
  200.8 0.5 multiply_reduce_fusion
  201.3 0.2 fusion.27
  201.6 1.0 fusion.18
  (47 shorter events, 1.2 us)
Async XLA Ops:
  6.5 77.9 %all-gather.3.cloned.1.call-start = ((), (), s32[]{:S(2)}) async-start(), calls=%async_computation.4 | async-start | bytes 2785280 | tf_op jit(solution)/shard_map/all_gather | solution.py:69
  66.5 17.9 %copy-start = (bf16[512,576]{0,1:T(8,128)(2,1)S(1)}, bf16[512,576]{0,1:T(8,128)(2,1)}, u32[]{:S(2)}) copy-start(bf16[512,576]{0,1:T(8,128)(2,1)} %param.10) | copy-start | bytes 1769476
  66.5 63.0 %all-to-all-start.2 = ((bf16[16,2,64,576]{3,2,1,0:T(8,128)(2,1)}), bf16[16,2,64,576]{3,2,1,0:T(8,128)(2,1)}, u32[]{:S(2)}, u32[]{:S(2)}) async-start(bf16[16,2,64,576]{3,2,1,0:T(8,128)(2,1)} %broadcast_select_fusion), calls=%async_computation.2 | async-start | bytes 5242880 | tf_op jit(solution)/shard_map/all_to_all | solution.py:106
  129.6 10.5 %all-to-all-start.1 = ((f32[16,1,128]{2,1,0:T(1,128)}), f32[16,1,128]{2,1,0:T(1,128)S(1)}, u32[]{:S(2)}, u32[]{:S(2)}) async-start(f32[16,1,128]{2,1,0:T(1,128)} %reshape.351), calls=%async_computation.1 | async-start | bytes 16384 | tf_op jit(solution)/shard_map/all_to_all | solution.py:117
  140.0 10.6 %all-to-all-start = ((f32[16,1,128]{2,1,0:T(1,128)}), f32[16,1,128]{2,1,0:T(1,128)S(1)}, u32[]{:S(2)}, u32[]{:S(2)}) async-start(f32[16,1,128]{2,1,0:T(1,128)} %reshape.349), calls=%async_computation | async-start | bytes 16384 | tf_op jit(solution)/shard_map/all_to_all | solution.py:118
  148.7 7.8 %copy-start.3 = (s32[1,2]{1,0:T(1,128)S(1)}, s32[1,2]{1,0:T(1,128)}, u32[]{:S(2)}) copy-start(s32[1,2]{1,0:T(1,128)} %param.15) | copy-start | bytes 28
  148.7 8.7 %copy-start.1 = (bf16[1,8,64,576]{3,2,1,0:T(8,128)(2,1)S(1)}, bf16[1,8,64,576]{3,2,1,0:T(8,128)(2,1)}, u32[]{:S(2)}) copy-start(bf16[1,8,64,576]{3,2,1,0:T(8,128)(2,1)} %param.11) | copy-start | bytes 1769476
  148.7 8.7 %copy-start.2 = (bf16[2,1,64,576]{3,2,1,0:T(8,128)(2,1)S(1)}, bf16[2,1,64,576]{3,2,1,0:T(8,128)(2,1)}, u32[]{:S(2)}) copy-start(bf16[2,1,64,576]{3,2,1,0:T(8,128)(2,1)} %param.9) | copy-start | bytes 442372
  148.7 8.7 %copy-start.4 = (bf16[2,1,576]{2,0,1:T(2,128)(2,1)S(1)}, bf16[2,1,576]{2,0,1:T(2,128)(2,1)}, u32[]{:S(2)}) copy-start(bf16[2,1,576]{2,0,1:T(2,128)(2,1)} %param.12) | copy-start | bytes 6916
  150.7 50.2 %all-to-all-start.3 = ((bf16[2,16,64,512]{3,2,0,1:T(8,128)(2,1)}), bf16[2,16,64,512]{3,2,0,1:T(8,128)(2,1)S(1)}, u32[]{:S(2)}, u32[]{:S(2)}) async-start(bf16[2,16,64,512]{3,2,0,1:T(8,128)(2,1)} %copy.25), calls=%async_computation.3 | async-start | bytes 4194304 | tf_op jit(solution)/shard_map/all_to_all | solution.py:114
Sparse Core Ops, SparseCore 0:
  10.1 74.2 all-gather.2
where the time goes:
time: 210 us; the launch traced here: 209 us
  waiting for transfers between devices  86 us (41%)
  blocking collectives  50.8 us (24%)
  starting transfers between devices  24 us (11%)
  between operations  14.9 us (7%)
  matrix products  14.2 us (7%)
  local copies, waits for them, and re-layouts  11.8 us (6%)
  other arithmetic  7.63 us (4%)
    all_to_all x1, waiting for transfers between devices, on_device(): lax.all_to_all(out_p.astype(jnp.float32), 'req', split_axis=1, concat_axi...  37.4 us
    all_to_all x1, waiting for transfers between devices, on_device(): lax.all_to_all(outgoing, 'req', split_axis=0, concat_axis=0, tiled=True)  30.9 us
    all_gather x1, blocking collectives, on_device(): lax.all_gather(fork_pages, 'req', axis=0, tiled=True)  30.8 us
    unnamed x1, blocking collectives  20 us
    all_gather x1, waiting for transfers between devices, on_device(): every_query = lax.all_gather(queries, 'req', axis=1, tiled=True)  10.9 us
    all_to_all x1, starting transfers between devices, on_device(): lax.all_to_all(outgoing, 'req', split_axis=0, concat_axis=0, tiled=True)  7.02 us
    dot_general x4, matrix products, prompt_block(): lax.dot_general(rows, keys, (((1,), (1,)), ((), ())), preferred_element_t...  6.88 us
    all_to_all x1, starting transfers between devices, on_device(): lax.all_to_all(out_p.astype(jnp.float32), 'req', split_axis=1, concat_axi...  5.88 us
  transfers between devices with their start and end apart: 5, of which 5 were waited for; matrix products, arithmetic and copies ran while one was open for 15% of the time, Pallas kernels for 0%

commit v1 on v0

v1 whole, which is shorter than its diff:
```python
import functools

import jax
import jax.numpy as jnp
from jax import lax
from jax.experimental import pallas as pl
from jax.experimental.pallas import tpu as pltpu
from jax.sharding import PartitionSpec as P

DL = 512
PLANE = 4

score_scale = 192.0 ** (-0.5)
neg_large = -1e30
MESH = pl.DeviceIdType.MESH
NT = (((1,), (1,)), ((), ()))


def kernel(
    col_n, head_n, steps_n, forks_n,
    q_hbm, prompt_hbm, suf_hbm, new_ref, len_ref, parent_ref, pages_ref,
    out_ref,
    q_all, prompt_all, suf_all, meta_own, meta_col, meta_plane, col_smem, plane_smem,
    top_ref, total_ref, acc_ref, out_send, stat_send, out_recv, stat_recv,
    local_sem, q_send, q_recv, mc_send, mc_recv, mp_send, mp_recv,
    p_send, p_recv, ps_send, ps_recv, s_send, s_recv, ss_send, ss_recv,
    o_send, o_recv, t_send, t_recv,
):
    req, head = lax.axis_index("req"), lax.axis_index("head")
    col, spot = req // PLANE, req % PLANE
    py, px = spot // 2, spot % 2
    odd = head % 2
    rows = q_hbm.shape[0]
    block = prompt_hbm.shape[0]
    pages_n, page_len, width = suf_hbm.shape
    own_n = pages_n * page_len
    piece, page_piece = block // head_n, pages_n // head_n

    def plane_peer(flip_y, flip_x):
        return col * PLANE + (py + flip_y * (1 - 2 * py)) * 2 + px + flip_x * (1 - 2 * px)

    first = plane_peer(odd, 1 - odd)
    second = plane_peer(1 - odd, odd)
    slot_first, slot_second = 1 + odd, 2 - odd

    def col_peer(shift):
        return ((col + shift + col_n) % col_n) * PLANE + spot

    def sib(shift):
        return (head + shift) % head_n

    def remote(src, dst, send, recv, to_req, to_head):
        return pltpu.make_async_remote_copy(
            src_ref=src, dst_ref=dst, send_sem=send, recv_sem=recv,
            device_id=(to_req, to_head), device_id_type=MESH,
        )

    barrier = pltpu.get_barrier_semaphore()
    for e in range(1, col_n):
        pl.semaphore_signal(barrier, inc=1, device_id=(col_peer(e), head), device_id_type=MESH)
    for d in range(1, PLANE):
        pl.semaphore_signal(
            barrier, inc=1, device_id=(plane_peer(d // 2, d % 2), head), device_id_type=MESH
        )
    for f in range(1, head_n):
        pl.semaphore_signal(barrier, inc=1, device_id=(req, sib(f)), device_id_type=MESH)

    q_here = pltpu.make_async_copy(q_hbm, q_all.at[pl.ds(0, rows)], local_sem.at[0])
    prompt_here = pltpu.make_async_copy(prompt_hbm, prompt_all.at[0], local_sem.at[1])
    suf_here = pltpu.make_async_copy(suf_hbm, suf_all.at[0], local_sem.at[2])
    q_here.start()
    prompt_here.start()
    suf_here.start()

    line = lax.broadcasted_iota(jnp.int32, (8, 128), 0)
    meta = jnp.where(line == 0, parent_ref[0], len_ref[0])
    for k in range(forks_n):
        meta = jnp.where(line == 2 + k, pages_ref[0, k], meta)
    meta_own[...] = meta
    meta_col[0] = meta
    meta_plane[0] = meta

    pl.semaphore_wait(barrier, col_n - 1 + PLANE - 1 + head_n - 1)

    sends = []

    def go(copy):
        copy.start()
        sends.append(copy)
        return copy

    def plane_send(hbm, every, part, send, recv):
        mine = pl.ds(head * part, part)
        return (
            go(remote(hbm.at[mine], every.at[slot_first, mine], send.at[0], recv.at[0], first, head)),
            go(remote(hbm.at[mine], every.at[slot_second, mine], send.at[1], recv.at[1], second, head)),
        )

    def sib_send(every, part, send, recv, kind, slot):
        mine = pl.ds(head * part, part)
        return [
            go(remote(
                every.at[slot, mine], every.at[slot, mine],
                send.at[f - 1, kind], recv.at[f - 1, kind], req, sib(f),
            ))
            for f in range(1, head_n)
        ]

    def pass_on(every, part, send, recv):
        mine = pl.ds(head * part, part)
        return go(remote(
            every.at[slot_first, mine], every.at[3, mine], send.at[2], recv.at[2], second, head
        ))

    p_copies = plane_send(prompt_hbm, prompt_all, piece, p_send, p_recv)
    q_copies = [
        go(remote(
            q_hbm, q_all.at[pl.ds(e * rows, rows)], q_send.at[e - 1], q_recv.at[e - 1],
            col_peer(e), head,
        ))
        for e in range(1, col_n)
    ]
    mc_copies = [
        go(remote(
            meta_own, meta_col.at[e], mc_send.at[e - 1], mc_recv.at[e - 1], col_peer(e), head
        ))
        for e in range(1, col_n)
    ]
    mp_copies = [
        go(remote(
            meta_own, meta_plane.at[d], mp_send.at[d - 1], mp_recv.at[d - 1],
            plane_peer(d // 2, d % 2), head,
        ))
        for d in range(1, PLANE)
    ]

    def attend(start, count, keys, valid=None, initial=False):
        there = pl.ds(start, count)
        scores = (
            lax.dot_general(q_all[there], keys, NT, preferred_element_type=jnp.float32)
            * score_scale
        )
        if valid is not None:
            scores = jnp.where(valid, scores, neg_large)
        top = jnp.max(scores, axis=-1, keepdims=True)
        if not initial:
            old = top_ref[there]
            top = jnp.maximum(top, old)
            factor = jnp.exp(old - top)
        weights = jnp.exp(scores - top)
        if valid is not None:
            weights = jnp.where(valid, weights, 0.0)
        total = jnp.sum(weights, axis=-1, keepdims=True)
        summed = jnp.dot(
            weights.astype(jnp.bfloat16), keys[:, :DL], preferred_element_type=jnp.float32
        )
        if not initial:
            total = total + total_ref[there] * factor
            summed = summed + acc_ref[there] * factor
        top_ref[there] = top
        total_ref[there] = total
        acc_ref[there] = summed

    q_here.wait()
    prompt_here.wait()
    attend(0, rows, prompt_all[0], initial=True)
    suf_here.wait()
    token = lax.broadcasted_iota(jnp.int32, (1, own_n), 1)
    attend(0, rows, suf_all[0].reshape(own_n, width), token < len_ref[0])
    fresh = new_ref[...].astype(jnp.float32)
    line_new = lax.broadcasted_iota(jnp.int32, (128, width), 0)
    new_keys = jnp.zeros((128, width), jnp.float32)
    for t in range(steps_n):
        new_keys = jnp.where(line_new == t, fresh[t : t + 1], new_keys)
    row = lax.broadcasted_iota(jnp.int32, (rows, 128), 0)
    lane = lax.broadcasted_iota(jnp.int32, (rows, 128), 1)
    attend(0, rows, new_keys.astype(jnp.bfloat16), lane <= row // (rows // steps_n))

    p_copies[0].wait_recv()
    p_pass = pass_on(prompt_all, piece, p_send, p_recv)
    sibs = sib_send(prompt_all, piece, ps_send, ps_recv, 0, slot_first)
    p_copies[1].wait_recv()
    sibs += sib_send(prompt_all, piece, ps_send, ps_recv, 1, slot_second)
    s_copies = plane_send(suf_hbm, suf_all, page_piece, s_send, s_recv)
    for copy in sibs:
        copy.wait_recv()
    attend(0, rows, prompt_all[1])
    attend(0, rows, prompt_all[2])
    p_pass.wait_recv()
    last_sibs = sib_send(prompt_all, piece, ps_send, ps_recv, 2, 3)

    others = (col_n - 1) * rows
    for copy in q_copies:
        copy.wait_recv()
    attend(rows, others, prompt_all[0], initial=True)
    for copy in last_sibs:
        copy.wait_recv()
    attend(0, rows, prompt_all[3])

    s_copies[0].wait_recv()
    s_pass = pass_on(suf_all, page_piece, s_send, s_recv)
    sibs = sib_send(suf_all, page_piece, ss_send, ss_recv, 0, slot_first)
    s_copies[1].wait_recv()
    sibs += sib_send(suf_all, page_piece, ss_send, ss_recv, 1, slot_second)
    attend(rows, others, prompt_all[1])
    attend(rows, others, prompt_all[2])
    s_pass.wait_recv()
    sibs += sib_send(suf_all, page_piece, ss_send, ss_recv, 2, 3)
    for copy in mc_copies + mp_copies:
        copy.wait_recv()
    col_down = pltpu.make_async_copy(meta_col, col_smem, local_sem.at[3])
    plane_down = pltpu.make_async_copy(meta_plane, plane_smem, local_sem.at[4])
    col_down.start()
    plane_down.start()
    attend(rows, others, prompt_all[3])
    col_down.wait()
    plane_down.wait()
    for copy in sibs:
        copy.wait_recv()

    diagonal = row == lane

    def as_line(column):
        return jnp.sum(jnp.where(diagonal, column, 0.0), axis=0, keepdims=True)

    def as_column(values):
        return jnp.sum(jnp.where(diagonal, values, 0.0), axis=1, keepdims=True)

    within = lax.broadcasted_iota(jnp.int32, (1, page_len), 1)

    def attend_fork(e):
        beam = col_smem[e, 0, 0]
        beam_col, beam_spot = beam // PLANE, beam % PLANE
        slot = jnp.abs(beam_spot % 2 - px) + 2 * jnp.abs(beam_spot // 2 - py)
        length = jnp.where(beam_col == col, plane_smem[slot, 1, 0], 0)
        keys = []
        for k in range(forks_n):
            page = col_smem[e, 2 + k, 0]
            keys.append(suf_all[slot, page])
        limit = jnp.concatenate(
            [within + col_smem[e, 2 + k, 0] * page_len for k in range(forks_n)], axis=1
        )
        attend(e * rows, rows, jnp.concatenate(keys, axis=0), limit < length)

    stat_line = lax.broadcasted_iota(jnp.int32, (8, 128), 0)
    back = []
    for e in range(1, col_n):
        attend_fork(e)
        there = pl.ds(e * rows, rows)
        top, total = top_ref[there], total_ref[there]
        out_send[e - 1] = (acc_ref[there] / total).astype(jnp.bfloat16)
        stat_send[e - 1] = jnp.where(stat_line == 0, as_line(top), as_line(total))
        back.append((
            go(remote(
                out_send.at[e - 1], out_recv.at[e - 1], o_send.at[e - 1], o_recv.at[e - 1],
                col_peer(-e), head,
            )),
            go(remote(
                stat_send.at[e - 1], stat_recv.at[e - 1], t_send.at[e - 1], t_recv.at[e - 1],
                col_peer(-e), head,
            )),
        ))
    attend_fork(0)

    here = pl.ds(0, rows)
    for e in range(1, col_n):
        for copy in back[e - 1]:
            copy.wait_recv()
        stats = stat_recv[e - 1]
        top_e, total_e = as_column(stats[0:1]), as_column(stats[1:2])
        old = top_ref[here]
        peak = jnp.maximum(old, top_e)
        keep, weight = jnp.exp(old - peak), total_e * jnp.exp(top_e - peak)
        top_ref[here] = peak
        total_ref[here] = total_ref[here] * keep + weight
        acc_ref[here] = acc_ref[here] * keep + out_recv[e - 1].astype(jnp.float32) * weight
    out_ref[...] = (acc_ref[here] / total_ref[here]).astype(jnp.bfloat16)
    for copy in sends:
        copy.wait_send()


def on_device(
    col_n, head_n, queries, prompt_cache, suffix_cache, new_latent, suffix_len, parent, fork_pages
):
    steps_n, beam_dev, head_dev, width = queries.shape
    pages_n, page_len = suffix_cache.shape[1:3]
    block = prompt_cache.shape[0]
    forks_n = fork_pages.shape[1]
    rows = steps_n * head_dev
    every = col_n * rows
    away = col_n - 1
    hbm = pl.BlockSpec(memory_space=pl.ANY)
    vmem = pl.BlockSpec(memory_space=pltpu.VMEM)
    smem = pl.BlockSpec(memory_space=pltpu.SMEM)
    dma = pltpu.SemaphoreType.DMA
    bf16, f32, i32 = jnp.bfloat16, jnp.float32, jnp.int32
    flops = 2 * every * PLANE * block * (width + DL)
    out = pl.pallas_call(
        functools.partial(kernel, col_n, head_n, steps_n, forks_n),
        out_shape=jax.ShapeDtypeStruct((rows, DL), bf16),
        in_specs=[hbm, hbm, hbm, vmem, smem, smem, smem],
        out_specs=vmem,
        scratch_shapes=[
            pltpu.VMEM((every, width), bf16),
            pltpu.VMEM((PLANE, block, width), bf16),
            pltpu.VMEM((PLANE, pages_n, page_len, width), bf16),
            pltpu.VMEM((8, 128), i32),
            pltpu.VMEM((col_n, 8, 128), i32),
            pltpu.VMEM((PLANE, 8, 128), i32),
            pltpu.SMEM((col_n, 8, 128), i32),
            pltpu.SMEM((PLANE, 8, 128), i32),
            pltpu.VMEM((every, 1), f32),
            pltpu.VMEM((every, 1), f32),
            pltpu.VMEM((every, DL), f32),
            pltpu.VMEM((away, rows, DL), bf16),
            pltpu.VMEM((away, 8, 128), f32),
            pltpu.VMEM((away, rows, DL), bf16),
            pltpu.VMEM((away, 8, 128), f32),
            dma((5,)),
            dma((away,)), dma((away,)),
            dma((away,)), dma((away,)),
            dma((PLANE - 1,)), dma((PLANE - 1,)),
            dma((3,)), dma((3,)),
            dma((head_n - 1, 3)), dma((head_n - 1, 3)),
            dma((3,)), dma((3,)),
            dma((head_n - 1, 3)), dma((head_n - 1, 3)),
            dma((away,)), dma((away,)),
            dma((away,)), dma((away,)),
        ],
        compiler_params=pltpu.CompilerParams(
            collective_id=0, has_side_effects=True, vmem_limit_bytes=48 * 1024 * 1024
        ),
        cost_estimate=pl.CostEstimate(
            flops=flops, bytes_accessed=4 * block * width, transcendentals=every * PLANE * block
        ),
    )(
        queries.reshape(rows, width),
        prompt_cache,
        suffix_cache.reshape(pages_n, page_len, width),
        new_latent.reshape(steps_n, width),
        suffix_len,
        parent,
        fork_pages,
    )
    return out.reshape(steps_n, beam_dev, head_dev, DL)


def solution(mesh):
    placed = (
        P(None, "req", "head", None),
        P("req", None),
        P("req", None, None, None),
        P(None, "req", None),
        P("req"),
        P("req"),
        P("req", None),
    )
    return jax.shard_map(
        functools.partial(on_device, mesh.shape["req"] // PLANE, mesh.shape["head"]),
        mesh=mesh,
        in_specs=placed,
        out_specs=P(None, "req", "head", None),
        check_vma=False,
    )
```

time: 210 us -> 50.3 us (0.24)
  the two profiles are of different devices: /device:TPU:12 before, /device:TPU:0 now
where the time goes in v1:
time: 50.3 us; the launch traced here: 50.1 us
  Pallas kernels  46.6 us (93%)
  local copies, waits for them, and re-layouts  2.07 us (4%)
  between operations  1.43 us (3%)
    pallas_call x1, Pallas kernels, on_device(): pl.pallas_call(functools.partial(kernel, col_n, head_n, steps_n, forks_n)...  46.6 us
    unnamed x10, local copies, waits for them, and re-layouts  2.07 us

profile of v1, /device:TPU:0, one launch (start us, length us, event | category | flops | bytes accessed | tf_op | source)
XLA Modules:
  0.0 50.1 jit_solution(14219685885653486819)
XLA Ops:
  0.0 0.0 copy-start
  1.4 0.0 copy-start.1
  1.4 0.0 copy-start.2
  1.4 0.0 copy-start.3
  1.4 1.4 %copy.8.prompt_hbm = bf16[512,576]{1,0:T(8,128)(2,1)S(1)} copy(bf16[512,576]{0,1:T(8,128)(2,1)} %param.8) | data formatting | bytes 1179648 | tf_op args[1]
  2.8 0.0 copy-done
  2.8 0.0 copy-done.1
  2.8 0.0 copy-done.2
  2.8 0.0 copy-done.3
  2.8 46.6 %shard_map.73 = bf16[128,512]{1,0:T(8,128)(2,1)S(1)} custom-call(bf16[128,576]{1,0:T(8,128)(2,1)S(1)} %bitcast.8, bf16[512,576]{1,0:T(8,128)(2,1)S(1)} %copy.8.prompt_hbm, bf16[8,64,576]{2,1,0:T(8,128)(2,1)S(1)} %bitcast.7, bf16[2,576]{1,0:T(2,128)(2,1)S(1)} %bitcast.9, s32[1]{0:T(128)S(6)} %copy.11.len_ref, s32[1]{0:T(128)S(6)} %copy.12.parent_ref, ...), custom_call_target="tpu_custom_call" | custom-call | flops 2281701376 | bytes 1179648 | tf_op jit(solution)/shard_map/pallas_call | solution.py:298
  49.4 0.7 %copy.13 = bf16[2,1,64,512]{3,2,1,0:T(8,128)(2,1)} copy(bf16[2,1,64,512]{3,2,1,0:T(8,128)(2,1)S(1)} %bitcast.6) | data formatting | bytes 262144
Async XLA Ops:
  0.0 2.8 %copy-start = (bf16[1,8,64,576]{3,2,1,0:T(8,128)(2,1)S(1)}, bf16[1,8,64,576]{3,2,1,0:T(8,128)(2,1)}, u32[]{:S(2)}) copy-start(bf16[1,8,64,576]{3,2,1,0:T(8,128)(2,1)} %param.9) | copy-start | bytes 1769476
  1.4 1.4 %copy-start.1 = (bf16[2,1,64,576]{3,2,1,0:T(8,128)(2,1)S(1)}, bf16[2,1,64,576]{3,2,1,0:T(8,128)(2,1)}, u32[]{:S(2)}) copy-start(bf16[2,1,64,576]{3,2,1,0:T(8,128)(2,1)} %param.7) | copy-start | bytes 442372
  1.4 1.4 %copy-start.2 = (bf16[2,1,576]{2,0,1:T(2,128)(2,1)S(1)}, bf16[2,1,576]{2,0,1:T(2,128)(2,1)}, u32[]{:S(2)}) copy-start(bf16[2,1,576]{2,0,1:T(2,128)(2,1)} %param.10) | copy-start | bytes 6916
  1.4 1.4 %copy-start.3 = (s32[1,2]{1,0:T(1,128)S(1)}, s32[1,2]{1,0:T(1,128)}, u32[]{:S(2)}) copy-start(s32[1,2]{1,0:T(1,128)} %pages_ref.1) | copy-start | bytes 28

commit v2 on v1

--- a/solution.py
+++ b/solution.py
@@ -1,4 +1,5 @@
 import functools
+import math
 
 import jax
 import jax.numpy as jnp
@@ -14,11 +15,12 @@
 neg_large = -1e30
 MESH = pl.DeviceIdType.MESH
 NT = (((1,), (1,)), ((), ()))
+NN = (((1,), (0,)), ((), ()))
 
 
 def kernel(
     col_n, head_n, steps_n, forks_n,
-    q_hbm, prompt_hbm, suf_hbm, new_ref, len_ref, parent_ref, pages_ref,
+    q_hbm, prompt_hbm, suf_hbm, new_ref, info_ref,
     out_ref,
     q_all, prompt_all, suf_all, meta_own, meta_col, meta_plane, col_smem, plane_smem,
     top_ref, total_ref, acc_ref, out_send, stat_send, out_recv, stat_recv,
@@ -31,10 +33,12 @@
     py, px = spot // 2, spot % 2
     odd = head % 2
     rows = q_hbm.shape[0]
-    block = prompt_hbm.shape[0]
+    width_n, block = prompt_hbm.shape
     pages_n, page_len, width = suf_hbm.shape
     own_n = pages_n * page_len
-    piece, page_piece = block // head_n, pages_n // head_n
+    parts = math.gcd(head_n, width_n // 16, pages_n)
+    piece, page_piece = width_n // parts, pages_n // parts
+    share, team = head % parts, head - head % parts
 
     def plane_peer(flip_y, flip_x):
         return col * PLANE + (py + flip_y * (1 - 2 * py)) * 2 + px + flip_x * (1 - 2 * px)
@@ -47,7 +51,7 @@
         return ((col + shift + col_n) % col_n) * PLANE + spot
 
     def sib(shift):
-        return (head + shift) % head_n
+        return team + (share + shift) % parts
 
     def remote(src, dst, send, recv, to_req, to_head):
         return pltpu.make_async_remote_copy(
@@ -62,7 +66,7 @@
         pl.semaphore_signal(
             barrier, inc=1, device_id=(plane_peer(d // 2, d % 2), head), device_id_type=MESH
         )
-    for f in range(1, head_n):
+    for f in range(1, parts):
         pl.semaphore_signal(barrier, inc=1, device_id=(req, sib(f)), device_id_type=MESH)
 
     q_here = pltpu.make_async_copy(q_hbm, q_all.at[pl.ds(0, rows)], local_sem.at[0])
@@ -73,14 +77,15 @@
     suf_here.start()
 
     line = lax.broadcasted_iota(jnp.int32, (8, 128), 0)
-    meta = jnp.where(line == 0, parent_ref[0], len_ref[0])
-    for k in range(forks_n):
-        meta = jnp.where(line == 2 + k, pages_ref[0, k], meta)
+    info = info_ref[...]
+    meta = jnp.zeros((8, 128), jnp.int32)
+    for k in range(2 + forks_n):
+        meta = jnp.where(line == k, info[:, k : k + 1], meta)
     meta_own[...] = meta
     meta_col[0] = meta
     meta_plane[0] = meta
 
-    pl.semaphore_wait(barrier, col_n - 1 + PLANE - 1 + head_n - 1)
+    pl.semaphore_wait(barrier, col_n - 1 + PLANE - 1 + parts - 1)
 
     sends = []
 
@@ -90,24 +95,24 @@
         return copy
 
     def plane_send(hbm, every, part, send, recv):
-        mine = pl.ds(head * part, part)
+        mine = pl.ds(share * part, part)
         return (
             go(remote(hbm.at[mine], every.at[slot_first, mine], send.at[0], recv.at[0], first, head)),
             go(remote(hbm.at[mine], every.at[slot_second, mine], send.at[1], recv.at[1], second, head)),
         )
 
     def sib_send(every, part, send, recv, kind, slot):
-        mine = pl.ds(head * part, part)
+        mine = pl.ds(share * part, part)
         return [
             go(remote(
                 every.at[slot, mine], every.at[slot, mine],
                 send.at[f - 1, kind], recv.at[f - 1, kind], req, sib(f),
             ))
-            for f in range(1, head_n)
+            for f in range(1, parts)
         ]
 
     def pass_on(every, part, send, recv):
-        mine = pl.ds(head * part, part)
+        mine = pl.ds(share * part, part)
         return go(remote(
             every.at[slot_first, mine], every.at[3, mine], send.at[2], recv.at[2], second, head
         ))
@@ -134,10 +139,12 @@
         for d in range(1, PLANE)
     ]
 
-    def attend(start, count, keys, valid=None, initial=False):
+    def attend(start, count, keys, valid=None, initial=False, turned=False):
         there = pl.ds(start, count)
         scores = (
-            lax.dot_general(q_all[there], keys, NT, preferred_element_type=jnp.float32)
+            lax.dot_general(
+                q_all[there], keys, NN if turned else NT, preferred_element_type=jnp.float32
+            )
             * score_scale
         )
         if valid is not None:
@@ -151,8 +158,11 @@
         if valid is not None:
             weights = jnp.where(valid, weights, 0.0)
         total = jnp.sum(weights, axis=-1, keepdims=True)
-        summed = jnp.dot(
-            weights.astype(jnp.bfloat16), keys[:, :DL], preferred_element_type=jnp.float32
+        summed = lax.dot_general(
+            weights.astype(jnp.bfloat16),
+            keys[:DL] if turned else keys[:, :DL],
+            NT if turned else NN,
+            preferred_element_type=jnp.float32,
         )
         if not initial:
             total = total + total_ref[there] * factor
@@ -161,12 +171,15 @@
         total_ref[there] = total
         acc_ref[there] = summed
 
+    def attend_prompt(start, count, slot, initial=False):
+        attend(start, count, prompt_all[slot], initial=initial, turned=True)
+
     q_here.wait()
     prompt_here.wait()
-    attend(0, rows, prompt_all[0], initial=True)
+    attend_prompt(0, rows, 0, initial=True)
     suf_here.wait()
     token = lax.broadcasted_iota(jnp.int32, (1, own_n), 1)
-    attend(0, rows, suf_all[0].reshape(own_n, width), token < len_ref[0])
+    attend(0, rows, suf_all[0].reshape(own_n, width), token < info[:, 1:2])
     fresh = new_ref[...].astype(jnp.float32)
     line_new = lax.broadcasted_iota(jnp.int32, (128, width), 0)
     new_keys = jnp.zeros((128, width), jnp.float32)
@@ -184,35 +197,43 @@
     s_copies = plane_send(suf_hbm, suf_all, page_piece, s_send, s_recv)
     for copy in sibs:
         copy.wait_recv()
-    attend(0, rows, prompt_all[1])
-    attend(0, rows, prompt_all[2])
+    attend_prompt(0, rows, 1)
+    attend_prompt(0, rows, 2)
     p_pass.wait_recv()
     last_sibs = sib_send(prompt_all, piece, ps_send, ps_recv, 2, 3)
 
-    others = (col_n - 1) * rows
+    group_n = math.gcd(col_n - 1, 3)
+    members = (col_n - 1) // group_n
+    many = members * rows
+
+    def group_start(g):
+        return (1 + g * members) * rows
+
     for copy in q_copies:
         copy.wait_recv()
-    attend(rows, others, prompt_all[0], initial=True)
+    attend_prompt(group_start(0), many, 0, initial=True)
+    attend_prompt(group_start(0), many, 1)
     for copy in last_sibs:
         copy.wait_recv()
-    attend(0, rows, prompt_all[3])
-
     s_copies[0].wait_recv()
     s_pass = pass_on(suf_all, page_piece, s_send, s_recv)
     sibs = sib_send(suf_all, page_piece, ss_send, ss_recv, 0, slot_first)
     s_copies[1].wait_recv()
     sibs += sib_send(suf_all, page_piece, ss_send, ss_recv, 1, slot_second)
-    attend(rows, others, prompt_all[1])
-    attend(rows, others, prompt_all[2])
-    s_pass.wait_recv()
-    sibs += sib_send(suf_all, page_piece, ss_send, ss_recv, 2, 3)
+    attend_prompt(group_start(0), many, 2)
+    attend_prompt(group_start(0), many, 3)
     for copy in mc_copies + mp_copies:
         copy.wait_recv()
     col_down = pltpu.make_async_copy(meta_col, col_smem, local_sem.at[3])
     plane_down = pltpu.make_async_copy(meta_plane, plane_smem, local_sem.at[4])
     col_down.start()
     plane_down.start()
-    attend(rows, others, prompt_all[3])
+    if group_n > 1:
+        for slot in range(PLANE):
+            attend_prompt(group_start(1), many, slot, initial=slot == 0)
+    s_pass.wait_recv()
+    sibs += sib_send(suf_all, page_piece, ss_send, ss_recv, 2, 3)
+    attend_prompt(0, rows, 3)
     col_down.wait()
     plane_down.wait()
     for copy in sibs:
@@ -245,6 +266,9 @@
     stat_line = lax.broadcasted_iota(jnp.int32, (8, 128), 0)
     back = []
     for e in range(1, col_n):
+        if e > 2 * members and (e - 1) % members == 0:
+            for slot in range(PLANE):
+                attend_prompt(group_start((e - 1) // members), many, slot, initial=slot == 0)
         attend_fork(e)
         there = pl.ds(e * rows, rows)
         top, total = top_ref[there], total_ref[there]
@@ -285,24 +309,25 @@
     steps_n, beam_dev, head_dev, width = queries.shape
     pages_n, page_len = suffix_cache.shape[1:3]
     block = prompt_cache.shape[0]
+    parts = math.gcd(head_n, width // 16, pages_n)
     forks_n = fork_pages.shape[1]
     rows = steps_n * head_dev
     every = col_n * rows
     away = col_n - 1
     hbm = pl.BlockSpec(memory_space=pl.ANY)
     vmem = pl.BlockSpec(memory_space=pltpu.VMEM)
-    smem = pl.BlockSpec(memory_space=pltpu.SMEM)
     dma = pltpu.SemaphoreType.DMA
     bf16, f32, i32 = jnp.bfloat16, jnp.float32, jnp.int32
     flops = 2 * every * PLANE * block * (width + DL)
+    info = jnp.concatenate([parent[:, None], suffix_len[:, None], fork_pages], axis=1)
     out = pl.pallas_call(
         functools.partial(kernel, col_n, head_n, steps_n, forks_n),
         out_shape=jax.ShapeDtypeStruct((rows, DL), bf16),
-        in_specs=[hbm, hbm, hbm, vmem, smem, smem, smem],
+        in_specs=[hbm, hbm, hbm, vmem, vmem],
         out_specs=vmem,
         scratch_shapes=[
             pltpu.VMEM((every, width), bf16),
-            pltpu.VMEM((PLANE, block, width), bf16),
+            pltpu.VMEM((PLANE, width, block), bf16),
             pltpu.VMEM((PLANE, pages_n, page_len, width), bf16),
             pltpu.VMEM((8, 128), i32),
             pltpu.VMEM((col_n, 8, 128), i32),
@@ -321,26 +346,24 @@
             dma((away,)), dma((away,)),
             dma((PLANE - 1,)), dma((PLANE - 1,)),
             dma((3,)), dma((3,)),
-            dma((head_n - 1, 3)), dma((head_n - 1, 3)),
+            dma((max(parts - 1, 1), 3)), dma((max(parts - 1, 1), 3)),
             dma((3,)), dma((3,)),
-            dma((head_n - 1, 3)), dma((head_n - 1, 3)),
+            dma((max(parts - 1, 1), 3)), dma((max(parts - 1, 1), 3)),
             dma((away,)), dma((away,)),
             dma((away,)), dma((away,)),
         ],
         compiler_params=pltpu.CompilerParams(
-            collective_id=0, has_side_effects=True, vmem_limit_bytes=48 * 1024 * 1024
+            collective_id=0, has_side_effects=True, vmem_limit_bytes=64 * 1024 * 1024
         ),
         cost_estimate=pl.CostEstimate(
             flops=flops, bytes_accessed=4 * block * width, transcendentals=every * PLANE * block
         ),
     )(
         queries.reshape(rows, width),
-        prompt_cache,
+        prompt_cache.T,
         suffix_cache.reshape(pages_n, page_len, width),
         new_latent.reshape(steps_n, width),
-        suffix_len,
-        parent,
-        fork_pages,
+        info,
     )
     return out.reshape(steps_n, beam_dev, head_dev, DL)
 

time: 50.3 us -> 51 us (1.014)
  other arithmetic: 0 us -> 0.65 us
    concatenate x0 -> x1, other arithmetic: none -> 0.65 us  [on_device(): jnp.concatenate([parent[:, None], suffix_len[:, None], fork_pages], axis=1)]
    unnamed x10 -> x3, local copies, waits for them, and re-layouts: 2.07 us -> 2.22 us
where the time goes in v2:
time: 51 us; the launch traced here: 50.8 us
  Pallas kernels  46.6 us (91%)
  local copies, waits for them, and re-layouts  2.22 us (4%)
  between operations  1.31 us (3%)
  other arithmetic  0.65 us (1%)
    pallas_call x1, Pallas kernels, on_device(): pl.pallas_call(functools.partial(kernel, col_n, head_n, steps_n, forks_n)...  46.6 us
    unnamed x3, local copies, waits for them, and re-layouts  2.22 us

profile of v2, /device:TPU:0, one launch (start us, length us, event | category | flops | bytes accessed | tf_op | source)
XLA Modules:
  0.0 50.8 jit_solution(709032541202685689)
XLA Ops:
  1.3 0.0 copy-start
  1.3 0.6 %copy-done = s32[1,2]{1,0:T(1,128)S(1)} copy-done((s32[1,2]{1,0:T(1,128)S(1)}, s32[1,2]{1,0:T(1,128)}, u32[]{:S(2)}) %copy-start) | copy-done | bytes 32
  2.0 0.7 %pad_add_fusion.info_ref = s32[1,4]{1,0:T(1,128)} fusion(s32[1,2]{1,0:T(1,128)S(1)} %copy-done, s32[1,1]{1,0:T(1,128)} %bitcast.9, s32[1,1]{1,0:T(1,128)} %bitcast.10), kind=kLoop, calls=%fused_computation | loop fusion | flops 8 | bytes 32 | tf_op jit(solution)/shard_map/concatenate | solution.py:322
  2.6 46.6 %shard_map.73 = bf16[128,512]{1,0:T(8,128)(2,1)} custom-call(bf16[128,576]{1,0:T(8,128)(2,1)} %bitcast.14, bf16[576,512]{1,0:T(8,128)(2,1)} %bitcast.13, bf16[8,64,576]{2,1,0:T(8,128)(2,1)} %bitcast.12, bf16[2,576]{1,0:T(2,128)(2,1)} %bitcast.15, s32[1,4]{1,0:T(1,128)} %pad_add_fusion.info_ref), custom_call_target="tpu_custom_call" | custom-call | flops 2281701376 | bytes 1179648 | tf_op jit(solution)/shard_map/pallas_call | solution.py:323
  49.2 1.6 %copy.12 = bf16[2,1,64,512]{3,2,1,0:T(8,128)(2,1)} copy(bf16[2,1,64,512]{3,2,1,0:T(8,128)(2,1)} %bitcast.11) | data formatting | bytes 262144
Async XLA Ops:
  1.3 0.7 %copy-start = (s32[1,2]{1,0:T(1,128)S(1)}, s32[1,2]{1,0:T(1,128)}, u32[]{:S(2)}) copy-start(s32[1,2]{1,0:T(1,128)} %param.13) | copy-start | bytes 28

commit v3 on v2

--- a/solution.py
+++ b/solution.py
@@ -20,7 +20,7 @@
 
 def kernel(
     col_n, head_n, steps_n, forks_n,
-    q_hbm, prompt_hbm, suf_hbm, new_ref, info_ref,
+    q_hbm, prompt_hbm, suf_hbm, new_ref, info_ref, pages_ref,
     out_ref,
     q_all, prompt_all, suf_all, meta_own, meta_col, meta_plane, col_smem, plane_smem,
     top_ref, total_ref, acc_ref, out_send, stat_send, out_recv, stat_recv,
@@ -78,9 +78,10 @@
 
     line = lax.broadcasted_iota(jnp.int32, (8, 128), 0)
     info = info_ref[...]
-    meta = jnp.zeros((8, 128), jnp.int32)
-    for k in range(2 + forks_n):
-        meta = jnp.where(line == k, info[:, k : k + 1], meta)
+    meta = jnp.where(line == 0, info[:, 0:1], info[:, 1:2])
+    pages = pages_ref[...]
+    for k in range(forks_n):
+        meta = jnp.where(line == 2 + k, pages[:, k : k + 1], meta)
     meta_own[...] = meta
     meta_col[0] = meta
     meta_plane[0] = meta
@@ -138,6 +139,8 @@
         ))
         for d in range(1, PLANE)
     ]
+
+    s_copies = plane_send(suf_hbm, suf_all, page_piece, s_send, s_recv)
 
     def attend(start, count, keys, valid=None, initial=False, turned=False):
         there = pl.ds(start, count)
@@ -194,49 +197,38 @@
     sibs = sib_send(prompt_all, piece, ps_send, ps_recv, 0, slot_first)
     p_copies[1].wait_recv()
     sibs += sib_send(prompt_all, piece, ps_send, ps_recv, 1, slot_second)
-    s_copies = plane_send(suf_hbm, suf_all, page_piece, s_send, s_recv)
     for copy in sibs:
         copy.wait_recv()
     attend_prompt(0, rows, 1)
     attend_prompt(0, rows, 2)
-    p_pass.wait_recv()
-    last_sibs = sib_send(prompt_all, piece, ps_send, ps_recv, 2, 3)
-
-    group_n = math.gcd(col_n - 1, 3)
-    members = (col_n - 1) // group_n
-    many = members * rows
-
-    def group_start(g):
-        return (1 + g * members) * rows
-
-    for copy in q_copies:
-        copy.wait_recv()
-    attend_prompt(group_start(0), many, 0, initial=True)
-    attend_prompt(group_start(0), many, 1)
-    for copy in last_sibs:
-        copy.wait_recv()
     s_copies[0].wait_recv()
     s_pass = pass_on(suf_all, page_piece, s_send, s_recv)
-    sibs = sib_send(suf_all, page_piece, ss_send, ss_recv, 0, slot_first)
+    s_sibs = sib_send(suf_all, page_piece, ss_send, ss_recv, 0, slot_first)
     s_copies[1].wait_recv()
-    sibs += sib_send(suf_all, page_piece, ss_send, ss_recv, 1, slot_second)
-    attend_prompt(group_start(0), many, 2)
-    attend_prompt(group_start(0), many, 3)
+    s_sibs += sib_send(suf_all, page_piece, ss_send, ss_recv, 1, slot_second)
+    p_pass.wait_recv()
+    sibs = sib_send(prompt_all, piece, ps_send, ps_recv, 2, 3)
+
+    others = (col_n - 1) * rows
+    for copy in q_copies:
+        copy.wait_recv()
+    attend_prompt(rows, others, 0, initial=True)
+    attend_prompt(rows, others, 1)
+    s_pass.wait_recv()
+    s_sibs += sib_send(suf_all, page_piece, ss_send, ss_recv, 2, 3)
     for copy in mc_copies + mp_copies:
         copy.wait_recv()
     col_down = pltpu.make_async_copy(meta_col, col_smem, local_sem.at[3])
     plane_down = pltpu.make_async_copy(meta_plane, plane_smem, local_sem.at[4])
     col_down.start()
     plane_down.start()
-    if group_n > 1:
-        for slot in range(PLANE):
-            attend_prompt(group_start(1), many, slot, initial=slot == 0)
-    s_pass.wait_recv()
-    sibs += sib_send(suf_all, page_piece, ss_send, ss_recv, 2, 3)
-    attend_prompt(0, rows, 3)
+    attend_prompt(rows, others, 2)
+    for copy in sibs:
+        copy.wait_recv()
+    attend_prompt(rows, others, 3)
     col_down.wait()
     plane_down.wait()
-    for copy in sibs:
+    for copy in s_sibs:
         copy.wait_recv()
 
     diagonal = row == lane
@@ -266,9 +258,6 @@
     stat_line = lax.broadcasted_iota(jnp.int32, (8, 128), 0)
     back = []
     for e in range(1, col_n):
-        if e > 2 * members and (e - 1) % members == 0:
-            for slot in range(PLANE):
-                attend_prompt(group_start((e - 1) // members), many, slot, initial=slot == 0)
         attend_fork(e)
         there = pl.ds(e * rows, rows)
         top, total = top_ref[there], total_ref[there]
@@ -284,6 +273,7 @@
                 col_peer(-e), head,
             )),
         ))
+    attend_prompt(0, rows, 3)
     attend_fork(0)
 
     here = pl.ds(0, rows)
@@ -319,11 +309,11 @@
     dma = pltpu.SemaphoreType.DMA
     bf16, f32, i32 = jnp.bfloat16, jnp.float32, jnp.int32
     flops = 2 * every * PLANE * block * (width + DL)
-    info = jnp.concatenate([parent[:, None], suffix_len[:, None], fork_pages], axis=1)
+    info = jnp.concatenate([parent[:, None], suffix_len[:, None]], axis=1)
     out = pl.pallas_call(
         functools.partial(kernel, col_n, head_n, steps_n, forks_n),
         out_shape=jax.ShapeDtypeStruct((rows, DL), bf16),
-        in_specs=[hbm, hbm, hbm, vmem, vmem],
+        in_specs=[hbm, hbm, hbm, vmem, vmem, vmem],
         out_specs=vmem,
         scratch_shapes=[
             pltpu.VMEM((every, width), bf16),
@@ -353,7 +343,7 @@
             dma((away,)), dma((away,)),
         ],
         compiler_params=pltpu.CompilerParams(
-            collective_id=0, has_side_effects=True, vmem_limit_bytes=64 * 1024 * 1024
+            collective_id=0, has_side_effects=True, vmem_limit_bytes=48 * 1024 * 1024
         ),
         cost_estimate=pl.CostEstimate(
             flops=flops, bytes_accessed=4 * block * width, transcendentals=every * PLANE * block
@@ -364,6 +354,7 @@
         suffix_cache.reshape(pages_n, page_len, width),
         new_latent.reshape(steps_n, width),
         info,
+        fork_pages,
     )
     return out.reshape(steps_n, beam_dev, head_dev, DL)
 

time: 51 us -> 50.4 us (0.988)
  Pallas kernels: 46.6 us -> 44.4 us
  local copies, waits for them, and re-layouts: 2.22 us -> 4.41 us
  other arithmetic: 0.65 us -> 0.07 us
    pallas_call x1, Pallas kernels: 46.6 us -> 44.4 us  [on_device(): pl.pallas_call(functools.partial(kernel, col_n, head_n, steps_n, forks_n)...]
    unnamed x3 -> x11, local copies, waits for them, and re-layouts: 2.22 us -> 4.41 us
    concatenate x1, other arithmetic: 0.65 us -> 0.07 us  [on_device(): info = jnp.concatenate([parent[:, None], suffix_len[:, None]], axis=1)]
where the time goes in v3:
time: 50.4 us; the launch traced here: 50.2 us
  Pallas kernels  44.4 us (88%)
  local copies, waits for them, and re-layouts  4.41 us (9%)
  between operations  1.31 us (3%)
    pallas_call x1, Pallas kernels, on_device(): pl.pallas_call(functools.partial(kernel, col_n, head_n, steps_n, forks_n)...  44.4 us
    unnamed x11, local copies, waits for them, and re-layouts  4.41 us

profile of v3, /device:TPU:0, one launch (start us, length us, event | category | flops | bytes accessed | tf_op | source)
XLA Modules:
  0.0 50.2 jit_solution(263954627825442351)
XLA Ops:
  1.3 0.1 pad_add_fusion.info_ref
  1.4 0.0 copy-start.3
  1.4 0.0 copy-start.4
  1.4 0.7 %copy-done.3 = bf16[2,1,576]{2,0,1:T(2,128)(2,1)S(1)} copy-done((bf16[2,1,576]{2,0,1:T(2,128)(2,1)S(1)}, bf16[2,1,576]{2,0,1:T(2,128)(2,1)}, u32[]{:S(2)}) %copy-start.3) | copy-done | bytes 2328
  2.1 0.0 copy-done.4
  2.1 0.0 copy-start
  2.1 1.1 %copy-done = bf16[1,8,64,576]{3,2,1,0:T(8,128)(2,1)S(1)} copy-done((bf16[1,8,64,576]{3,2,1,0:T(8,128)(2,1)S(1)}, bf16[1,8,64,576]{3,2,1,0:T(8,128)(2,1)}, u32[]{:S(2)}) %copy-start) | copy-done | bytes 589848
  3.1 0.0 copy-start.1
  3.1 1.1 %copy-done.1 = bf16[512,576]{0,1:T(8,128)(2,1)S(1)} copy-done((bf16[512,576]{0,1:T(8,128)(2,1)S(1)}, bf16[512,576]{0,1:T(8,128)(2,1)}, u32[]{:S(2)}) %copy-start.1) | copy-done | bytes 589848
  4.2 0.0 copy-start.2
  4.2 0.9 %copy-done.2 = bf16[2,1,64,576]{3,2,1,0:T(8,128)(2,1)S(1)} copy-done((bf16[2,1,64,576]{3,2,1,0:T(8,128)(2,1)S(1)}, bf16[2,1,64,576]{3,2,1,0:T(8,128)(2,1)}, u32[]{:S(2)}) %copy-start.2) | copy-done | bytes 147480
  5.1 44.4 %shard_map.73 = bf16[128,512]{1,0:T(8,128)(2,1)S(1)} custom-call(bf16[128,576]{1,0:T(8,128)(2,1)S(1)} %bitcast.14, bf16[576,512]{1,0:T(8,128)(2,1)S(1)} %bitcast.13, bf16[8,64,576]{2,1,0:T(8,128)(2,1)S(1)} %bitcast.12, bf16[2,576]{1,0:T(2,128)(2,1)S(1)} %bitcast.15, s32[1,2]{1,0:T(1,128)S(1)} %pad_add_fusion.info_ref, s32[1,2]{1,0:T(1,128)S(1)} %copy-done.4), custom_call_target="tpu_custom_call" | custom-call | flops 2281701376 | bytes 1179648 | tf_op jit(solution)/shard_map/pallas_call | solution.py:313
  49.5 0.7 %copy.12 = bf16[2,1,64,512]{3,2,1,0:T(8,128)(2,1)} copy(bf16[2,1,64,512]{3,2,1,0:T(8,128)(2,1)S(1)} %bitcast.11) | data formatting | bytes 262144
Async XLA Ops:
  1.4 0.7 %copy-start.3 = (bf16[2,1,576]{2,0,1:T(2,128)(2,1)S(1)}, bf16[2,1,576]{2,0,1:T(2,128)(2,1)}, u32[]{:S(2)}) copy-start(bf16[2,1,576]{2,0,1:T(2,128)(2,1)} %param.10) | copy-start | bytes 6916
  1.4 0.7 %copy-start.4 = (s32[1,2]{1,0:T(1,128)S(1)}, s32[1,2]{1,0:T(1,128)}, u32[]{:S(2)}) copy-start(s32[1,2]{1,0:T(1,128)} %pages_ref.1) | copy-start | bytes 28
  2.1 1.1 %copy-start = (bf16[1,8,64,576]{3,2,1,0:T(8,128)(2,1)S(1)}, bf16[1,8,64,576]{3,2,1,0:T(8,128)(2,1)}, u32[]{:S(2)}) copy-start(bf16[1,8,64,576]{3,2,1,0:T(8,128)(2,1)} %param.9) | copy-start | bytes 1769476
  3.1 1.1 %copy-start.1 = (bf16[512,576]{0,1:T(8,128)(2,1)S(1)}, bf16[512,576]{0,1:T(8,128)(2,1)}, u32[]{:S(2)}) copy-start(bf16[512,576]{0,1:T(8,128)(2,1)} %param.8) | copy-start | bytes 1769476
  4.2 0.9 %copy-start.2 = (bf16[2,1,64,576]{3,2,1,0:T(8,128)(2,1)S(1)}, bf16[2,1,64,576]{3,2,1,0:T(8,128)(2,1)}, u32[]{:S(2)}) copy-start(bf16[2,1,64,576]{3,2,1,0:T(8,128)(2,1)} %param.7) | copy-start | bytes 442372

commit v4 on v3

--- a/solution.py
+++ b/solution.py
@@ -197,22 +197,20 @@
     sibs = sib_send(prompt_all, piece, ps_send, ps_recv, 0, slot_first)
     p_copies[1].wait_recv()
     sibs += sib_send(prompt_all, piece, ps_send, ps_recv, 1, slot_second)
-    for copy in sibs:
-        copy.wait_recv()
-    attend_prompt(0, rows, 1)
-    attend_prompt(0, rows, 2)
     s_copies[0].wait_recv()
     s_pass = pass_on(suf_all, page_piece, s_send, s_recv)
     s_sibs = sib_send(suf_all, page_piece, ss_send, ss_recv, 0, slot_first)
     s_copies[1].wait_recv()
     s_sibs += sib_send(suf_all, page_piece, ss_send, ss_recv, 1, slot_second)
     p_pass.wait_recv()
-    sibs = sib_send(prompt_all, piece, ps_send, ps_recv, 2, 3)
+    last_sibs = sib_send(prompt_all, piece, ps_send, ps_recv, 2, 3)
 
     others = (col_n - 1) * rows
     for copy in q_copies:
         copy.wait_recv()
     attend_prompt(rows, others, 0, initial=True)
+    for copy in sibs:
+        copy.wait_recv()
     attend_prompt(rows, others, 1)
     s_pass.wait_recv()
     s_sibs += sib_send(suf_all, page_piece, ss_send, ss_recv, 2, 3)
@@ -223,7 +221,7 @@
     col_down.start()
     plane_down.start()
     attend_prompt(rows, others, 2)
-    for copy in sibs:
+    for copy in last_sibs:
         copy.wait_recv()
     attend_prompt(rows, others, 3)
     col_down.wait()
@@ -273,7 +271,8 @@
                 col_peer(-e), head,
             )),
         ))
-    attend_prompt(0, rows, 3)
+    for slot in range(1, PLANE):
+        attend_prompt(0, rows, slot)
     attend_fork(0)
 
     here = pl.ds(0, rows)
@@ -304,7 +303,7 @@
     rows = steps_n * head_dev
     every = col_n * rows
     away = col_n - 1
-    hbm = pl.BlockSpec(memory_space=pl.ANY)
+    hbm = pl.BlockSpec(memory_space=pltpu.HBM)
     vmem = pl.BlockSpec(memory_space=pltpu.VMEM)
     dma = pltpu.SemaphoreType.DMA
     bf16, f32, i32 = jnp.bfloat16, jnp.float32, jnp.int32

time: 50.4 us -> 50.4 us (level)
  no operation moved by 1% of the time
where the time goes in v4:
time: 50.4 us; the launch traced here: 50.2 us
  Pallas kernels  44.4 us (88%)
  local copies, waits for them, and re-layouts  4.41 us (9%)
  between operations  1.31 us (3%)
    pallas_call x1, Pallas kernels, on_device(): pl.pallas_call(functools.partial(kernel, col_n, head_n, steps_n, forks_n)...  44.4 us
    unnamed x11, local copies, waits for them, and re-layouts  4.41 us

profile of v4, /device:TPU:0, one launch (start us, length us, event | category | flops | bytes accessed | tf_op | source)
XLA Modules:
  0.0 50.2 jit_solution(11875513425398355240)
XLA Ops:
  1.3 0.1 pad_add_fusion.info_ref
  1.4 0.0 copy-start.3
  1.4 0.0 copy-start.4
  1.4 0.7 %copy-done.3 = bf16[2,1,576]{2,0,1:T(2,128)(2,1)S(1)} copy-done((bf16[2,1,576]{2,0,1:T(2,128)(2,1)S(1)}, bf16[2,1,576]{2,0,1:T(2,128)(2,1)}, u32[]{:S(2)}) %copy-start.3) | copy-done | bytes 2328
  2.1 0.0 copy-done.4
  2.1 0.0 copy-start
  2.1 1.1 %copy-done = bf16[1,8,64,576]{3,2,1,0:T(8,128)(2,1)S(1)} copy-done((bf16[1,8,64,576]{3,2,1,0:T(8,128)(2,1)S(1)}, bf16[1,8,64,576]{3,2,1,0:T(8,128)(2,1)}, u32[]{:S(2)}) %copy-start) | copy-done | bytes 589848
  3.1 0.0 copy-start.1
  3.1 1.1 %copy-done.1 = bf16[512,576]{0,1:T(8,128)(2,1)S(1)} copy-done((bf16[512,576]{0,1:T(8,128)(2,1)S(1)}, bf16[512,576]{0,1:T(8,128)(2,1)}, u32[]{:S(2)}) %copy-start.1) | copy-done | bytes 589848
  4.2 0.0 copy-start.2
  4.2 0.9 %copy-done.2 = bf16[2,1,64,576]{3,2,1,0:T(8,128)(2,1)S(1)} copy-done((bf16[2,1,64,576]{3,2,1,0:T(8,128)(2,1)S(1)}, bf16[2,1,64,576]{3,2,1,0:T(8,128)(2,1)}, u32[]{:S(2)}) %copy-start.2) | copy-done | bytes 147480
  5.1 44.4 %shard_map.73 = bf16[128,512]{1,0:T(8,128)(2,1)S(1)} custom-call(bf16[128,576]{1,0:T(8,128)(2,1)S(1)} %bitcast.14, bf16[576,512]{1,0:T(8,128)(2,1)S(1)} %bitcast.13, bf16[8,64,576]{2,1,0:T(8,128)(2,1)S(1)} %bitcast.12, bf16[2,576]{1,0:T(2,128)(2,1)S(1)} %bitcast.15, s32[1,2]{1,0:T(1,128)S(1)} %pad_add_fusion.info_ref, s32[1,2]{1,0:T(1,128)S(1)} %copy-done.4), custom_call_target="tpu_custom_call" | custom-call | flops 2281701376 | bytes 1179648 | tf_op jit(solution)/shard_map/pallas_call | solution.py:312
  49.5 0.7 %copy.12 = bf16[2,1,64,512]{3,2,1,0:T(8,128)(2,1)} copy(bf16[2,1,64,512]{3,2,1,0:T(8,128)(2,1)S(1)} %bitcast.11) | data formatting | bytes 262144
Async XLA Ops:
  1.4 0.7 %copy-start.3 = (bf16[2,1,576]{2,0,1:T(2,128)(2,1)S(1)}, bf16[2,1,576]{2,0,1:T(2,128)(2,1)}, u32[]{:S(2)}) copy-start(bf16[2,1,576]{2,0,1:T(2,128)(2,1)} %param.10) | copy-start | bytes 6916
  1.4 0.7 %copy-start.4 = (s32[1,2]{1,0:T(1,128)S(1)}, s32[1,2]{1,0:T(1,128)}, u32[]{:S(2)}) copy-start(s32[1,2]{1,0:T(1,128)} %pages_ref.1) | copy-start | bytes 28
  2.1 1.1 %copy-start = (bf16[1,8,64,576]{3,2,1,0:T(8,128)(2,1)S(1)}, bf16[1,8,64,576]{3,2,1,0:T(8,128)(2,1)}, u32[]{:S(2)}) copy-start(bf16[1,8,64,576]{3,2,1,0:T(8,128)(2,1)} %param.9) | copy-start | bytes 1769476
  3.1 1.1 %copy-start.1 = (bf16[512,576]{0,1:T(8,128)(2,1)S(1)}, bf16[512,576]{0,1:T(8,128)(2,1)}, u32[]{:S(2)}) copy-start(bf16[512,576]{0,1:T(8,128)(2,1)} %param.8) | copy-start | bytes 1769476
  4.2 0.9 %copy-start.2 = (bf16[2,1,64,576]{3,2,1,0:T(8,128)(2,1)S(1)}, bf16[2,1,64,576]{3,2,1,0:T(8,128)(2,1)}, u32[]{:S(2)}) copy-start(bf16[2,1,64,576]{3,2,1,0:T(8,128)(2,1)} %param.7) | copy-start | bytes 442372
